TPU v7x, 512 devices: a whole 4x4x16 slice. The times are simulated.
512 devices in a mesh: ma: 32 (over z, core), row: 16 (over y, x).
Axes of the slice: x: 4, y: 4, z: 16, core: 2. Of those that a mesh axis runs over, the one named last changes fastest.
Arguments:
- seed_field: bfloat16 [4, 16, 2, 1024, 1024], P(None, 'row', None, 'ma'), may hold values from -6 to 6
- cotangent: bfloat16 [2, 16, 2, 1024, 1024], P(None, 'row', None, 'ma'), may hold values from -6 to 6
- step_size: float32 [1], replicated, may hold values from 0.25 to 1
- owner_list: int32 [1024], replicated, may hold values from 0 to 1023, as said below
Outputs:
- nonlinear: float32 [2, 16, 2, 1024, 1024], P(None, 'row', None, 'ma')
- seed_next: float32 [4, 16, 2, 1024, 1024], P(None, 'row', None, 'ma')
Inputs may be any that keep to these rules, and one draw needn't show every extreme that they name: owner_list is a permutation of the wavenumbers; entries 32 d to 32 (d + 1) - 1 name the wavenumbers of owner d, and a block that holds m also holds 1023 - m.
All inputs are finite; a program needn't handle non-finite values.
Results may differ from a plain program's by a relative error of at most 0.0082.
Values may be sent and summed in bfloat16 or wider, within the bound.
A program may use at most 64 MiB of HBM per device.

v0:
```python
import math
import jax
import jax.numpy as jnp
from jax import lax
from jax.sharding import PartitionSpec as P

WAVES = 1024
DEGREES = 1024
NLAT = 1024
NLON = 2048


def with_halo(cells, sides, width):
    for axis, dim in sides:
        count = lax.axis_size(axis)
        ends = count - 1
        head = lax.slice_in_dim(cells, 0, width, axis=dim)
        tail = lax.slice_in_dim(cells, cells.shape[dim] - width, cells.shape[dim], axis=dim)
        cells = jnp.concatenate(
            [
                lax.ppermute(tail, axis, [(i, (i + 1) % count) for i in range(ends)]),
                cells,
                lax.ppermute(head, axis, [((i + 1) % count, i) for i in range(ends)]),
            ],
            axis=dim,
        )
    return cells


def lat_cosines(theta_index):
    degree = jnp.arange(DEGREES, dtype=jnp.int32)
    phase_index = (2 * theta_index[:, None] + 1) * degree[None, :] % (4 * NLAT)
    return jnp.cos(phase_index.astype(jnp.float32) * (math.pi / (2 * NLAT))).astype(jnp.bfloat16)


def wave_cosines(wave_ids):
    points = jnp.arange(NLON, dtype=jnp.int32)
    phase_index = wave_ids[:, None] * points[None, :] % NLON
    angles = phase_index.astype(jnp.float32) * (2.0 * math.pi / NLON)
    return jnp.stack([jnp.cos(angles), -jnp.sin(angles)]).astype(jnp.bfloat16)


def local(seed_field, cotangent, step_size, owner_list):
    own_waves = cotangent.shape[3]
    norm_scale = 2.0 / math.sqrt(DEGREES * WAVES)
    block_width = min(128, WAVES)
    my_waves = lax.dynamic_slice_in_dim(owner_list, lax.axis_index("ma") * own_waves, own_waves)
    degree = jnp.arange(DEGREES, dtype=jnp.int32)
    live_cols = degree[:, None] >= my_waves[None, :]
    live_rows = jnp.transpose(live_cols)
    zero_value = jnp.zeros((), jnp.bfloat16)
    listed = jnp.take(seed_field, owner_list, axis=4)
    owned_seed = lax.all_to_all(listed, "ma", split_axis=4, concat_axis=3, tiled=True)
    lat_table = lat_cosines(jnp.arange(NLAT, dtype=jnp.int32))
    forward_rows = jnp.einsum(
        "crslk,tl->crstk",
        jnp.where(live_cols, owned_seed, zero_value),
        lat_table,
        preferred_element_type=jnp.float32,
    )
    adjoint_rows = jnp.einsum(
        "crskl,tl->crstk",
        jnp.where(live_rows, cotangent, zero_value),
        lat_table,
        preferred_element_type=jnp.float32,
    )
    spec_rows = jnp.concatenate([forward_rows, adjoint_rows], axis=0).astype(jnp.bfloat16)
    gridded = lax.all_to_all(spec_rows, "ma", split_axis=3, concat_axis=4, tiled=True)
    grid_field = None
    for start in range(0, WAVES, block_width):
        wave_block = wave_cosines(owner_list[start : start + block_width])
        partial_grid = jnp.einsum(
            "crsjm,smf->crjf",
            gridded[..., start : start + block_width],
            wave_block,
            preferred_element_type=jnp.float32,
        )
        grid_field = partial_grid if grid_field is None else grid_field + partial_grid
    grid_field = norm_scale * grid_field
    radial_pair = jnp.stack([grid_field[1], grid_field[3]])
    padded = with_halo(radial_pair, (("row", 1),), 1)
    slopes = 0.5 * (padded[:, 2:] - padded[:, :-2])
    vel_tor = grid_field[0]
    mag_tor = grid_field[2]
    adj_vel = grid_field[4]
    adj_mag = grid_field[5]
    vel_pol = slopes[0]
    mag_pol = slopes[1]
    term_vel = mag_tor * mag_pol - vel_tor * vel_pol
    term_mag = vel_tor * mag_pol - vel_pol * mag_tor
    grad_vtor = -vel_pol * adj_vel + mag_pol * adj_mag
    grad_vpol = -vel_tor * adj_vel - mag_tor * adj_mag
    grad_mtor = mag_pol * adj_vel - vel_pol * adj_mag
    grad_mpol = mag_tor * adj_vel + vel_tor * adj_mag
    cotangent_pair = jnp.stack([grad_vpol, grad_mpol])
    padded_back = with_halo(cotangent_pair, (("row", 1),), 1)
    back_slopes = 0.5 * (padded_back[:, :-2] - padded_back[:, 2:])
    analysis_in = jnp.stack(
        [term_vel, term_mag, grad_vtor, back_slopes[0], grad_mtor, back_slopes[1]]
    ).astype(jnp.bfloat16)
    spectra_parts = []
    for start in range(0, WAVES, block_width):
        wave_block = wave_cosines(owner_list[start : start + block_width])
        spectra_parts.append(
            jnp.einsum(
                "crjf,smf->crsjm", analysis_in, wave_block, preferred_element_type=jnp.float32
            )
        )
    spectra = (norm_scale * jnp.concatenate(spectra_parts, axis=4)).astype(jnp.bfloat16)
    position = jnp.arange(NLAT, dtype=jnp.int32)
    returned = lax.all_to_all(spectra, "ma", split_axis=4, concat_axis=3, tiled=True)
    back_table = lat_cosines(position)
    result = jnp.einsum("crstk,tl->crskl", returned, back_table, preferred_element_type=jnp.float32)
    result = jnp.where(live_rows, result, 0.0)
    nonlinear = result[:2]
    seed_next = jnp.swapaxes(owned_seed, 3, 4).astype(jnp.float32) - step_size[0] * result[2:]
    return (nonlinear, seed_next)


def solution(mesh):
    return jax.shard_map(
        local,
        mesh=mesh,
        in_specs=(P(None, "row", None, "ma", None), P(None, "row", None, "ma", None), P(), P()),
        out_specs=(P(None, "row", None, "ma", None), P(None, "row", None, "ma", None)),
        check_vma=False,
    )
```

profile of v0, /device:TPU:15, one launch (start us, length us, event | category | flops | bytes accessed | tf_op | source)
XLA Modules:
  0.0 314.3 jit_solution(7844892380250730172)
XLA Ops:
  0.6 0.7 compare_and_fusion
  1.3 0.7 fusion.140
  2.0 2.8 copy.26
  4.9 8.9 %gather_fusion = bf16[1024,4,2,32]{3,1,2,0:T(4,128)(2,1)} fusion(bf16[4,2,32,1024]{2,0,3,1:T(4,128)(2,1)S(1)} %bitcast.362, s32[1024]{0:T(1024)S(1)} %fusion.140), kind=kCustom, calls=%fused_computation | custom fusion | bytes 1052672 | tf_op jit(solution)/shard_map/jit(_take)/gather | solution.py:52
  13.7 5.2 %fusion.173 = bf16[1024,1,2,4,32]{4,3,2,1,0:T(4,128)(2,1)S(1)} fusion(bf16[1024,4,2,32]{3,1,2,0:T(4,128)(2,1)} %gather_fusion, pred[1024]{0:T(1024)(128)(4,1)S(1)} %compare_and_fusion), kind=kLoop, calls=%fused_computation.271 | loop fusion | flops 262144 | bytes 1049600
  19.0 2.7 reshape.1275
  21.7 16.6 %all-to-all-start = ((bf16[32,2,4096]{2,1,0:T(2,128)(2,1)}), bf16[32,2,4096]{2,1,0:T(2,128)(2,1)S(1)}, u32[]{:S(2)}, u32[]{:S(2)}) async-start(bf16[32,2,4096]{2,1,0:T(2,128)(2,1)} %reshape.1275), calls=%async_computation | async-start | bytes 1048576 | tf_op jit(solution)/shard_map/all_to_all | solution.py:53
  38.5 16.2 %fusion.45 = bf16[2,1,2,1024,32]{3,4,2,0,1:T(8,128)(2,1)S(1)} fusion(s32[1024]{0:T(1024)S(1)} %multiply_add_fusion.1, bf16[2,1,2,32,1024]{4,3,2,1,0:T(8,128)(2,1)S(1)} %copy-done.18, pred[32,1024]{1,0:T(8,128)(4,1)S(1)} %iota_compare_fusion.1), kind=kOutput, calls=%fused_computation.75 | convolution fusion | flops 284426240 | bytes 561152 | tf_op jit(solution)/shard_map/crskl,tl->crstk/dot_general | solution.py:61
  54.7 16.9 %all-to-all-done = bf16[32,2,4096]{2,1,0:T(2,128)(2,1)S(1)} async-done(((bf16[32,2,4096]{2,1,0:T(2,128)(2,1)}), bf16[32,2,4096]{2,1,0:T(2,128)(2,1)S(1)}, u32[]{:S(2)}, u32[]{:S(2)}) %all-to-all-start) | async-done | bytes 524320 | tf_op jit(solution)/shard_map/all_to_all | solution.py:53
  71.6 1.0 reshape.1276
  72.7 4.0 %fusion.171 = (f32[4,1,2,32,32,32]{4,3,5,2,0,1:T(8,128)}, bf16[4,1,2,32,32,32]{4,3,5,2,0,1:T(8,128)(2,1)}) fusion(bf16[4,1,2,32,32,32]{3,0,2,5,4,1:T(4,128)(2,1)S(1)} %bitcast.361), kind=kLoop, calls=%fused_computation.269 | loop fusion | flops 262144 | bytes 2097152 | tf_op jit(solution)/shard_map/convert_element_type | solution.py:116
  76.7 3.5 %all_to_all.40 = bf16[4,2,1024,32]{2,3,1,0:T(8,128)(2,1)S(1)} reshape(bf16[4,1,2,32,32,32]{4,3,5,2,0,1:T(8,128)(2,1)} %get-tuple-element.11) | data formatting | bytes 1048576 | tf_op jit(solution)/shard_map/all_to_all | solution.py:53
  80.2 16.3 %fusion.39 = bf16[4,1,2,1024,32]{3,4,2,0,1:T(8,128)(2,1)S(1)} fusion(s32[1024]{0:T(1024)S(1)} %multiply_add_fusion.1, bf16[4,2,1024,32]{2,3,1,0:T(8,128)(2,1)S(1)} %all_to_all.40, pred[1024,32]{0,1:T(8,128)(4,1)S(1)} %iota_compare_fusion), kind=kOutput, calls=%fused_computation.73 | convolution fusion | flops 553123840 | bytes 1085440 | tf_op jit(solution)/shard_map/crslk,tl->crstk/dot_general | solution.py:55
  96.5 0.9 pad_maximum_fusion.8
  97.5 6.8 %copy.29 = bf16[6,1,2,1024,32]{4,2,0,1,3:T(2,128)(2,1)S(1)} copy(bf16[6,1,2,1024,32]{3,4,2,0,1:T(8,128)(2,1)} %pad_maximum_fusion.8) | data formatting | bytes 1572864 | tf_op jit(solution)/shard_map/concatenate | solution.py:67
  104.3 3.7 %reshape.1277 = bf16[32,2,6144]{2,1,0:T(2,128)(2,1)} reshape(bf16[1024,1,6,2,32]{4,3,2,1,0:T(2,128)(2,1)S(1)} %bitcast.359) | data formatting | bytes 1572864
  108.0 5.1 %all-to-all-start.1 = ((bf16[32,2,6144]{2,1,0:T(2,128)(2,1)}), bf16[32,2,6144]{2,1,0:T(2,128)(2,1)}, u32[]{:S(2)}, u32[]{:S(2)}) async-start(bf16[32,2,6144]{2,1,0:T(2,128)(2,1)} %reshape.1277), calls=%async_computation.1 | async-start | bytes 1572864 | tf_op jit(solution)/shard_map/all_to_all | solution.py:68
  113.1 9.9 %cosine_convert_fusion.6 = (bf16[1,128,2048]{2,1,0:T(8,128)(2,1)}, bf16[1,128,2048]{2,1,0:T(8,128)(2,1)}, bf16[1,128,2048]{2,1,0:T(8,128)(2,1)}, bf16[1,128,2048]{2,1,0:T(8,128)(2,1)}) fusion(s32[128]{0:T(128)S(1)} %get-tuple-element.19, s32[128]{0:T(128)S(1)} %get-tuple-element.16), kind=kLoop, calls=%fused_computation.169 | loop fusion | flops 8912896 | bytes 2098176 | tf_op jit(solution)/shard_map/convert.28
  123.0 9.9 %cosine_convert_fusion.4 = (bf16[1,128,2048]{2,1,0:T(8,128)(2,1)}, bf16[1,128,2048]{2,1,0:T(8,128)(2,1)}, bf16[1,128,2048]{2,1,0:T(8,128)(2,1)}, bf16[1,128,2048]{2,1,0:T(8,128)(2,1)}) fusion(s32[128]{0:T(128)S(1)} %get-tuple-element.17, s32[128]{0:T(128)S(1)} %get-tuple-element.18), kind=kLoop, calls=%fused_computation.161 | loop fusion | flops 8912896 | bytes 2098176 | tf_op jit(solution)/shard_map/convert.24
  132.8 9.8 %cosine_convert_fusion.2 = (bf16[1,128,2048]{2,1,0:T(8,128)(2,1)}, bf16[1,128,2048]{2,1,0:T(8,128)(2,1)}, bf16[1,128,2048]{2,1,0:T(8,128)(2,1)}, bf16[1,128,2048]{2,1,0:T(8,128)(2,1)}) fusion(s32[128]{0:T(128)S(1)} %get-tuple-element.21, s32[128]{0:T(128)S(1)} %get-tuple-element.20), kind=kLoop, calls=%fused_computation.153 | loop fusion | flops 8912896 | bytes 2098176 | tf_op jit(solution)/shard_map/convert.20
  142.7 9.8 %cosine_convert_fusion = (bf16[1,128,2048]{2,1,0:T(8,128)(2,1)}, bf16[1,128,2048]{2,1,0:T(8,128)(2,1)}, bf16[1,128,2048]{2,1,0:T(8,128)(2,1)}, bf16[1,128,2048]{2,1,0:T(8,128)(2,1)}) fusion(s32[128]{0:T(128)S(1)} %get-tuple-element.22, s32[128]{0:T(128)S(1)} %get-tuple-element.23), kind=kLoop, calls=%fused_computation.145 | loop fusion | flops 8912896 | bytes 2098176 | tf_op jit(solution)/shard_map/convert.16
  152.5 5.1 %all-to-all-done.1 = bf16[32,2,6144]{2,1,0:T(2,128)(2,1)} async-done(((bf16[32,2,6144]{2,1,0:T(2,128)(2,1)}), bf16[32,2,6144]{2,1,0:T(2,128)(2,1)}, u32[]{:S(2)}, u32[]{:S(2)}) %all-to-all-start.1) | async-done | bytes 786464 | tf_op jit(solution)/shard_map/all_to_all | solution.py:68
  157.6 7.2 %reshape.1278 = bf16[1024,1,6,2,32]{4,3,2,1,0:T(2,128)(2,1)S(1)} reshape(bf16[32,2,6144]{2,1,0:T(2,128)(2,1)} %all-to-all-done.1) | data formatting | bytes 1572864
  164.8 3.7 %copy.58 = bf16[6,1,2,32,32,32]{5,3,4,2,0,1:T(8,128)(2,1)} copy(bf16[6,1,2,32,32,32]{5,2,0,4,3,1:T(2,128)(2,1)S(1)} %bitcast.355) | data formatting | bytes 1572864 | tf_op jit(solution)/shard_map/all_to_all | solution.py:68
  168.5 5.3 %all_to_all.44 = bf16[6,1,2,32,1024]{4,3,2,0,1:T(8,128)(2,1)S(1)} reshape(bf16[6,1,2,32,32,32]{5,4,3,2,0,1:T(8,128)(2,1)} %bitcast.356) | data formatting | bytes 1572864 | tf_op jit(solution)/shard_map/all_to_all | solution.py:68
  173.9 0.4 convolution_bitcast_fusion
  174.3 0.6 copy-done.11
  175.0 0.4 convolution_bitcast_fusion.1
  175.5 0.4 convolution_bitcast_fusion.2
  175.9 0.3 copy-done.9
  176.3 0.4 convolution_bitcast_fusion.3
  176.7 0.4 convolution_bitcast_fusion.4
  177.1 0.3 copy-done.13
  177.6 0.4 convolution_bitcast_fusion.5
  178.0 0.4 convolution_bitcast_fusion.6
  178.4 0.3 copy-done.15
  178.9 0.8 fusion.15
  179.7 3.1 collective-permute-start.1
  182.9 2.2 collective-permute-start
  185.1 2.5 collective-permute-start.3
  187.6 4.9 %collective-permute-start.2 = (f32[2,1,32,2048]{3,2,1,0:T(8,128)S(1)}, f32[2,1,32,2048]{3,2,1,0:T(8,128)S(1)}, u32[]{:S(2)}, u32[]{:S(2)}) collective-permute-start(f32[2,1,32,2048]{3,2,1,0:T(8,128)S(1)} %pad_maximum_fusion.26), channel_id=1, source_target_pairs={{0,1},{1,2},{2,3},{3,4},{4,5},{5,6},{6,7},{7,8},{8,9},{9,10},{10,1... | collective-permute-start | bytes 1572872 | tf_op jit(solution)/shard_map/ppermute | solution.py:21
  192.6 1.5 collective-permute-done.1
  194.1 5.0 %collective-permute-done = f32[2,1,32,2048]{3,2,1,0:T(8,128)S(1)} collective-permute-done((f32[2,1,32,2048]{3,2,1,0:T(8,128)S(1)}, f32[2,1,32,2048]{3,2,1,0:T(8,128)S(1)}, u32[]{:S(2)}, u32[]{:S(2)}) %collective-permute-start) | collective-permute-done | bytes 524320 | tf_op jit(solution)/shard_map/ppermute | solution.py:23
  199.3 11.0 %collective-permute-done.3 = f32[2,1,32,2048]{3,2,1,0:T(8,128)S(1)} collective-permute-done((f32[2,1,32,2048]{3,2,1,0:T(8,128)S(1)}, f32[2,1,32,2048]{3,2,1,0:T(8,128)S(1)}, u32[]{:S(2)}, u32[]{:S(2)}) %collective-permute-start.3) | collective-permute-done | bytes 524320 | tf_op jit(solution)/shard_map/ppermute | solution.py:23
  210.4 0.5 fusion.55
  210.9 0.5 fusion.54
  211.4 0.5 fusion.53
  211.9 0.5 fusion.52
  212.5 0.5 fusion.51
  213.0 0.5 fusion.50
  213.5 0.5 fusion.49
  214.0 0.5 fusion.48
  214.5 1.0 multiply_convert_fusion
  215.5 6.8 %copy.31 = bf16[6,1,2,32,1024]{3,2,1,0,4:T(2,128)(2,1)S(1)} copy(bf16[6,1,2,32,1024]{4,3,0,2,1:T(8,128)(2,1)} %multiply_convert_fusion) | data formatting | bytes 1572864 | tf_op jit(solution)/shard_map/convert_element_type | solution.py:109
  222.4 3.7 %reshape.1279 = bf16[32,2,6144]{2,1,0:T(2,128)(2,1)} reshape(bf16[1024,6,1,2,32]{4,3,2,1,0:T(2,128)(2,1)S(1)} %bitcast.360) | data formatting | bytes 1572864
  226.1 9.4 %all-to-all-start.2 = ((bf16[32,2,6144]{2,1,0:T(2,128)(2,1)}), bf16[32,2,6144]{2,1,0:T(2,128)(2,1)}, u32[]{:S(2)}, u32[]{:S(2)}) async-start(bf16[32,2,6144]{2,1,0:T(2,128)(2,1)} %reshape.1279), calls=%async_computation.2 | async-start | bytes 1572864 | tf_op jit(solution)/shard_map/all_to_all | solution.py:111
  236.2 4.6 %reshape.1245 = f32[4,1,2,1024,32]{3,4,2,0,1:T(8,128)} reshape(f32[4,1,2,32,32,32]{4,3,5,2,0,1:T(8,128)} %get-tuple-element.10) | data formatting | bytes 2097152 | tf_op jit(solution)/shard_map/convert_element_type | solution.py:116
  240.7 39.3 %all-to-all-done.2 = bf16[32,2,6144]{2,1,0:T(2,128)(2,1)} async-done(((bf16[32,2,6144]{2,1,0:T(2,128)(2,1)}), bf16[32,2,6144]{2,1,0:T(2,128)(2,1)}, u32[]{:S(2)}, u32[]{:S(2)}) %all-to-all-start.2) | async-done | bytes 786464 | tf_op jit(solution)/shard_map/all_to_all | solution.py:111
  280.0 7.2 %reshape.1280 = bf16[1024,6,1,2,32]{4,3,2,1,0:T(2,128)(2,1)S(1)} reshape(bf16[32,2,6144]{2,1,0:T(2,128)(2,1)} %all-to-all-done.2) | data formatting | bytes 1572864
  287.2 3.7 %copy.57 = bf16[6,1,2,32,32,32]{3,4,5,2,0,1:T(8,128)(2,1)} copy(bf16[6,1,2,32,32,32]{3,2,0,5,4,1:T(2,128)(2,1)S(1)} %bitcast.357) | data formatting | bytes 1572864 | tf_op jit(solution)/shard_map/all_to_all | solution.py:111
  290.9 5.0 %reshape.1244 = bf16[6,2,1024,32]{2,3,1,0:T(8,128)(2,1)S(1)} reshape(bf16[6,1,2,32,32,32]{4,3,5,2,0,1:T(8,128)(2,1)} %bitcast.358) | data formatting | bytes 1572864 | tf_op jit(solution)/shard_map/reshape.39
  296.0 16.2 %fusion.33 = f32[6,2,32,1024]{3,2,1,0:T(8,128)S(1)} fusion(bf16[6,2,1024,32]{2,3,1,0:T(8,128)(2,1)S(1)} %reshape.1244, s32[1024]{0:T(1024)S(1)} %multiply_add_fusion.1, pred[32,1024]{1,0:T(8,128)(4,1)S(1)} %iota_compare_fusion.1), kind=kOutput, calls=%fused_computation.71 | convolution fusion | flops 821428224 | bytes 2396160 | tf_op jit(solution)/shard_map/crstk,tl->crskl/dot_general | solution.py:113
  312.1 0.8 slice_bitcast_fusion
  312.9 1.1 fusion.82
  (52 shorter events, 1.5 us)
Async XLA Ops:
  19.0 19.3 %copy-start.17 = (s32[1024]{0:T(1024)S(1)}, s32[1024]{0:T(1024)}, u32[]{:S(2)}) copy-start(s32[1024]{0:T(1024)} %param.7) | copy-start | bytes 12292
  19.0 19.6 %copy-start.18 = (bf16[2,1,2,32,1024]{4,3,2,1,0:T(8,128)(2,1)S(1)}, bf16[2,1,2,32,1024]{4,3,2,1,0:T(8,128)(2,1)}, u32[]{:S(2)}) copy-start(bf16[2,1,2,32,1024]{4,3,2,1,0:T(8,128)(2,1)} %param.5) | copy-start | bytes 786436
  21.7 50.0 %all-to-all-start = ((bf16[32,2,4096]{2,1,0:T(2,128)(2,1)}), bf16[32,2,4096]{2,1,0:T(2,128)(2,1)S(1)}, u32[]{:S(2)}, u32[]{:S(2)}) async-start(bf16[32,2,4096]{2,1,0:T(2,128)(2,1)} %reshape.1275), calls=%async_computation | async-start | bytes 1048576 | tf_op jit(solution)/shard_map/all_to_all | solution.py:53
  108.0 49.6 %all-to-all-start.1 = ((bf16[32,2,6144]{2,1,0:T(2,128)(2,1)}), bf16[32,2,6144]{2,1,0:T(2,128)(2,1)}, u32[]{:S(2)}, u32[]{:S(2)}) async-start(bf16[32,2,6144]{2,1,0:T(2,128)(2,1)} %reshape.1277), calls=%async_computation.1 | async-start | bytes 1572864 | tf_op jit(solution)/shard_map/all_to_all | solution.py:68
  168.5 5.3 %copy-start.3 = (bf16[1,128,2048]{2,1,0:T(8,128)(2,1)S(1)}, bf16[1,128,2048]{2,1,0:T(8,128)(2,1)}, u32[]{:S(2)}) copy-start(bf16[1,128,2048]{2,1,0:T(8,128)(2,1)} %get-tuple-element.38) | copy-start | bytes 1572868
  168.5 5.4 %copy-start.4 = (bf16[1,128,2048]{2,1,0:T(8,128)(2,1)S(1)}, bf16[1,128,2048]{2,1,0:T(8,128)(2,1)}, u32[]{:S(2)}) copy-start(bf16[1,128,2048]{2,1,0:T(8,128)(2,1)} %get-tuple-element.39) | copy-start | bytes 1572868
  173.8 1.0 copy-start.11
  173.8 1.2 copy-start.12
  173.9 1.6 copy-start.1
  173.9 1.6 copy-start.2
  175.0 1.1 copy-start.9
  175.0 1.3 copy-start.10
  175.4 1.2 copy-start.5
  175.5 1.3 copy-start.6
  176.3 1.1 copy-start.13
  176.3 1.3 copy-start.14
  176.7 1.2 copy-start.7
  176.7 1.3 copy-start.8
  177.6 1.1 copy-start.15
  177.6 1.3 copy-start.16
  179.7 14.3 %collective-permute-start.1 = (f32[2,1,32,2048]{3,2,1,0:T(8,128)S(1)}, f32[2,1,32,2048]{3,2,1,0:T(8,128)S(1)}, u32[]{:S(2)}, u32[]{:S(2)}) collective-permute-start(f32[2,1,32,2048]{3,2,1,0:T(8,128)S(1)} %pad_maximum_fusion.25), channel_id=1, source_target_pairs={{0,1},{1,2},{2,3},{3,4},{4,5},{5,6},{6,7},{7,8},{8,9},{9,10},{10,1... | collective-permute-start | bytes 1572872 | tf_op jit(solution)/shard_map/ppermute | solution.py:21
  182.9 16.2 %collective-permute-start = (f32[2,1,32,2048]{3,2,1,0:T(8,128)S(1)}, f32[2,1,32,2048]{3,2,1,0:T(8,128)S(1)}, u32[]{:S(2)}, u32[]{:S(2)}) collective-permute-start(f32[2,1,32,2048]{3,2,1,0:T(8,128)S(1)} %pad_maximum_fusion.25), channel_id=1, source_target_pairs={{1,0},{2,1},{3,2},{4,3},{5,4},{6,5},{7,6},{8,7},{9,8},{10,9},{11,1... | collective-permute-start | bytes 1572872 | tf_op jit(solution)/shard_map/ppermute | solution.py:23
  185.1 25.1 %collective-permute-start.3 = (f32[2,1,32,2048]{3,2,1,0:T(8,128)S(1)}, f32[2,1,32,2048]{3,2,1,0:T(8,128)S(1)}, u32[]{:S(2)}, u32[]{:S(2)}) collective-permute-start(f32[2,1,32,2048]{3,2,1,0:T(8,128)S(1)} %pad_maximum_fusion.26), channel_id=1, source_target_pairs={{1,0},{2,1},{3,2},{4,3},{5,4},{6,5},{7,6},{8,7},{9,8},{10,9},{11,1... | collective-permute-start | bytes 1572872 | tf_op jit(solution)/shard_map/ppermute | solution.py:23
  187.6 22.6 %collective-permute-start.2 = (f32[2,1,32,2048]{3,2,1,0:T(8,128)S(1)}, f32[2,1,32,2048]{3,2,1,0:T(8,128)S(1)}, u32[]{:S(2)}, u32[]{:S(2)}) collective-permute-start(f32[2,1,32,2048]{3,2,1,0:T(8,128)S(1)} %pad_maximum_fusion.26), channel_id=1, source_target_pairs={{0,1},{1,2},{2,3},{3,4},{4,5},{5,6},{6,7},{7,8},{8,9},{9,10},{10,1... | collective-permute-start | bytes 1572872 | tf_op jit(solution)/shard_map/ppermute | solution.py:21
  226.1 53.9 %all-to-all-start.2 = ((bf16[32,2,6144]{2,1,0:T(2,128)(2,1)}), bf16[32,2,6144]{2,1,0:T(2,128)(2,1)}, u32[]{:S(2)}, u32[]{:S(2)}) async-start(bf16[32,2,6144]{2,1,0:T(2,128)(2,1)} %reshape.1279), calls=%async_computation.2 | async-start | bytes 1572864 | tf_op jit(solution)/shard_map/all_to_all | solution.py:111
  295.9 17.0 %copy-start = (f32[4,1,2,1024,32]{3,4,2,0,1:T(8,128)S(1)}, f32[4,1,2,1024,32]{3,4,2,0,1:T(8,128)}, u32[]{:S(2)}) copy-start(f32[4,1,2,1024,32]{3,4,2,0,1:T(8,128)} %reshape.1245) | copy-start | bytes 3145732
where the time goes:
time: 319 us; the launch traced here: 314 us
  local copies, waits for them, and re-layouts  79.9 us (25%)
  waiting for transfers between devices  78.8 us (25%)
  matrix products  56.2 us (18%)
  other arithmetic  53.7 us (17%)
  starting transfers between devices  43.7 us (14%)
    another operation x5, other arithmetic  39.4 us
    all_to_all x1, waiting for transfers between devices, local(): lax.all_to_all(spectra, 'ma', split_axis=4, concat_axis=3, tiled=True)  39.3 us
    unnamed x47, local copies, waits for them, and re-layouts  31.5 us
    all_to_all x1, waiting for transfers between devices, local(): lax.all_to_all(listed, 'ma', split_axis=4, concat_axis=3, tiled=True)  16.9 us
    all_to_all x1, starting transfers between devices, local(): lax.all_to_all(listed, 'ma', split_axis=4, concat_axis=3, tiled=True)  16.6 us
    dot_general x1, matrix products, local(): jnp.einsum('crslk,tl->crstk', jnp.where(live_cols, owned_seed, zero_value...  16.3 us
    dot_general x1, matrix products, local(): jnp.einsum('crskl,tl->crstk', jnp.where(live_rows, cotangent, zero_value)...  16.2 us
    dot_general x1, matrix products, local(): jnp.einsum('crstk,tl->crskl', returned, back_table, preferred_element_typ...  16.2 us
  transfers between devices with their start and end apart: 7, of which 6 were waited for; matrix products, arithmetic and copies ran while one was open for 19% of the time, Pallas kernels for 0%

commit v1 on v0

--- a/solution.py
+++ b/solution.py
@@ -65,7 +65,9 @@
         preferred_element_type=jnp.float32,
     )
     spec_rows = jnp.concatenate([forward_rows, adjoint_rows], axis=0).astype(jnp.bfloat16)
-    gridded = lax.all_to_all(spec_rows, "ma", split_axis=3, concat_axis=4, tiled=True)
+    cells_2 = jnp.split(spec_rows, lax.axis_size("ma"), axis=3)
+    arrived = lax.all_to_all(jnp.stack(cells_2), "ma", 0, 0)
+    gridded = jnp.concatenate(arrived, axis=4)
     grid_field = None
     for start in range(0, WAVES, block_width):
         wave_block = wave_cosines(owner_list[start : start + block_width])

time: 319 us -> 312 us (0.978)
  local copies, waits for them, and re-layouts: 79.9 us -> 71.5 us
    reshape x0 -> x3, local copies, waits for them, and re-layouts: none -> 13.1 us  [local(): gridded = jnp.concatenate(arrived, axis=4)]
    all_to_all x2 -> x0, local copies, waits for them, and re-layouts: 9 us -> none  [local(): lax.all_to_all(spec_rows, 'ma', split_axis=3, concat_axis=4, tiled=True)]
    concatenate x1 -> x0, local copies, waits for them, and re-layouts: 6.79 us -> none  [local(): jnp.concatenate([forward_rows, adjoint_rows], axis=0).astype(jnp.bfloat16)]
    unnamed x47, local copies, waits for them, and re-layouts: 31.5 us -> 25.8 us
    unnamed x6 -> x37, other arithmetic: 6.59 us -> 9.6 us
    another operation x5 -> x6, other arithmetic: 39.4 us -> 39.5 us
  transfers between devices with their start and end apart: 7 -> 7, of which waited for: 6 -> 6; matrix products, arithmetic and copies ran while one was open for 19% -> 20% of each run, Pallas kernels for 0% -> 0%
where the time goes in v1:
time: 312 us; the launch traced here: 308 us
  waiting for transfers between devices  79.1 us (25%)
  local copies, waits for them, and re-layouts  71.5 us (23%)
  matrix products  56.2 us (18%)
  other arithmetic  55.9 us (18%)
  starting transfers between devices  42.8 us (14%)
    all_to_all x1, waiting for transfers between devices, local(): lax.all_to_all(spectra, 'ma', split_axis=4, concat_axis=3, tiled=True)  39.5 us
    another operation x5, other arithmetic  39.4 us
    unnamed x47, local copies, waits for them, and re-layouts  25.8 us
    all_to_all x1, waiting for transfers between devices, local(): lax.all_to_all(listed, 'ma', split_axis=4, concat_axis=3, tiled=True)  16.9 us
    all_to_all x1, starting transfers between devices, local(): lax.all_to_all(listed, 'ma', split_axis=4, concat_axis=3, tiled=True)  16.6 us
    dot_general x1, matrix products, local(): jnp.einsum('crslk,tl->crstk', jnp.where(live_cols, owned_seed, zero_value...  16.3 us
    dot_general x1, matrix products, local(): jnp.einsum('crskl,tl->crstk', jnp.where(live_rows, cotangent, zero_value)...  16.2 us
    dot_general x1, matrix products, local(): jnp.einsum('crstk,tl->crskl', returned, back_table, preferred_element_typ...  16.1 us
  transfers between devices with their start and end apart: 7, of which 6 were waited for; matrix products, arithmetic and copies ran while one was open for 20% of the time, Pallas kernels for 0%

profile of v1, /device:TPU:15, one launch (start us, length us, event | category | flops | bytes accessed | tf_op | source)
XLA Modules:
  0.0 307.7 jit_solution(15249829411751887190)
XLA Ops:
  0.6 0.7 compare_and_fusion
  1.3 0.7 fusion.173
  2.0 2.8 copy.24
  4.9 8.9 %gather_fusion = bf16[1024,4,2,32]{3,1,2,0:T(4,128)(2,1)} fusion(bf16[4,2,32,1024]{2,0,3,1:T(4,128)(2,1)S(1)} %bitcast.425, s32[1024]{0:T(1024)S(1)} %fusion.173), kind=kCustom, calls=%fused_computation | custom fusion | bytes 1052672 | tf_op jit(solution)/shard_map/jit(_take)/gather | solution.py:52
  13.7 5.3 %fusion.206 = bf16[1024,1,2,4,32]{4,3,2,1,0:T(4,128)(2,1)S(1)} fusion(bf16[1024,4,2,32]{3,1,2,0:T(4,128)(2,1)} %gather_fusion, pred[1024]{0:T(1024)(128)(4,1)S(1)} %compare_and_fusion), kind=kLoop, calls=%fused_computation.397 | loop fusion | flops 262144 | bytes 1049600
  19.0 2.7 reshape.1283
  21.7 16.6 %all-to-all-start = ((bf16[32,2,4096]{2,1,0:T(2,128)(2,1)}), bf16[32,2,4096]{2,1,0:T(2,128)(2,1)S(1)}, u32[]{:S(2)}, u32[]{:S(2)}) async-start(bf16[32,2,4096]{2,1,0:T(2,128)(2,1)} %reshape.1283), calls=%async_computation | async-start | bytes 1048576 | tf_op jit(solution)/shard_map/all_to_all | solution.py:53
  38.6 16.2 %fusion.45 = bf16[2,1,2,1024,32]{3,4,2,0,1:T(8,128)(2,1)S(1)} fusion(s32[1024]{0:T(1024)S(1)} %multiply_add_fusion.1, bf16[2,1,2,32,1024]{4,3,2,1,0:T(8,128)(2,1)S(1)} %copy-done.18, pred[32,1024]{1,0:T(8,128)(4,1)S(1)} %iota_compare_fusion.1), kind=kOutput, calls=%fused_computation.136 | convolution fusion | flops 284426240 | bytes 561152 | tf_op jit(solution)/shard_map/crskl,tl->crstk/dot_general | solution.py:61
  54.8 16.9 %all-to-all-done = bf16[32,2,4096]{2,1,0:T(2,128)(2,1)S(1)} async-done(((bf16[32,2,4096]{2,1,0:T(2,128)(2,1)}), bf16[32,2,4096]{2,1,0:T(2,128)(2,1)S(1)}, u32[]{:S(2)}, u32[]{:S(2)}) %all-to-all-start) | async-done | bytes 524320 | tf_op jit(solution)/shard_map/all_to_all | solution.py:53
  71.7 1.0 reshape.1284
  72.7 4.0 %fusion.204 = (f32[4,1,2,32,32,32]{4,3,5,2,0,1:T(8,128)}, bf16[4,1,2,32,32,32]{4,3,5,2,0,1:T(8,128)(2,1)}) fusion(bf16[4,1,2,32,32,32]{3,0,2,5,4,1:T(4,128)(2,1)S(1)} %bitcast.423), kind=kLoop, calls=%fused_computation.394 | loop fusion | flops 262144 | bytes 2097152 | tf_op jit(solution)/shard_map/convert_element_type | solution.py:118
  76.7 3.5 %all_to_all.30 = bf16[4,2,1024,32]{2,3,1,0:T(8,128)(2,1)S(1)} reshape(bf16[4,1,2,32,32,32]{4,3,5,2,0,1:T(8,128)(2,1)} %get-tuple-element.11) | data formatting | bytes 1048576 | tf_op jit(solution)/shard_map/all_to_all | solution.py:53
  80.2 16.3 %fusion.39 = bf16[4,1,2,1024,32]{3,4,2,0,1:T(8,128)(2,1)S(1)} fusion(s32[1024]{0:T(1024)S(1)} %multiply_add_fusion.1, bf16[4,2,1024,32]{2,3,1,0:T(8,128)(2,1)S(1)} %all_to_all.30, pred[1024,32]{0,1:T(8,128)(4,1)S(1)} %iota_compare_fusion), kind=kOutput, calls=%fused_computation.134 | convolution fusion | flops 553123840 | bytes 1085440 | tf_op jit(solution)/shard_map/crslk,tl->crstk/dot_general | solution.py:55
  99.7 3.7 %reshape.1285 = bf16[32,2,6144]{2,1,0:T(2,128)(2,1)} reshape(bf16[32,1,6,2,32,32]{5,4,3,2,1,0:T(8,128)(2,1)S(1)} %bitcast.424) | data formatting | bytes 1572864
  103.5 4.5 %all-to-all-start.1 = ((bf16[32,2,6144]{2,1,0:T(2,128)(2,1)}), bf16[32,2,6144]{2,1,0:T(2,128)(2,1)S(1)}, u32[]{:S(2)}, u32[]{:S(2)}) async-start(bf16[32,2,6144]{2,1,0:T(2,128)(2,1)} %reshape.1285), calls=%async_computation.1 | async-start | bytes 1572864 | tf_op jit(solution)/shard_map/all_to_all | solution.py:69
  107.9 9.9 %cosine_convert_fusion.6 = (bf16[1,128,2048]{2,1,0:T(8,128)(2,1)}, bf16[1,128,2048]{2,1,0:T(8,128)(2,1)}, bf16[1,128,2048]{2,1,0:T(8,128)(2,1)}, bf16[1,128,2048]{2,1,0:T(8,128)(2,1)}) fusion(s32[128]{0:T(128)S(1)} %get-tuple-element.19, s32[128]{0:T(128)S(1)} %get-tuple-element.16), kind=kLoop, calls=%fused_computation.230 | loop fusion | flops 8912896 | bytes 2098176 | tf_op jit(solution)/shard_map/convert.28
  117.8 9.9 %cosine_convert_fusion.4 = (bf16[1,128,2048]{2,1,0:T(8,128)(2,1)}, bf16[1,128,2048]{2,1,0:T(8,128)(2,1)}, bf16[1,128,2048]{2,1,0:T(8,128)(2,1)}, bf16[1,128,2048]{2,1,0:T(8,128)(2,1)}) fusion(s32[128]{0:T(128)S(1)} %get-tuple-element.17, s32[128]{0:T(128)S(1)} %get-tuple-element.18), kind=kLoop, calls=%fused_computation.222 | loop fusion | flops 8912896 | bytes 2098176 | tf_op jit(solution)/shard_map/convert.24
  127.7 9.8 %cosine_convert_fusion.2 = (bf16[1,128,2048]{2,1,0:T(8,128)(2,1)}, bf16[1,128,2048]{2,1,0:T(8,128)(2,1)}, bf16[1,128,2048]{2,1,0:T(8,128)(2,1)}, bf16[1,128,2048]{2,1,0:T(8,128)(2,1)}) fusion(s32[128]{0:T(128)S(1)} %get-tuple-element.21, s32[128]{0:T(128)S(1)} %get-tuple-element.20), kind=kLoop, calls=%fused_computation.214 | loop fusion | flops 8912896 | bytes 2098176 | tf_op jit(solution)/shard_map/convert.20
  137.5 9.8 %cosine_convert_fusion = (bf16[1,128,2048]{2,1,0:T(8,128)(2,1)}, bf16[1,128,2048]{2,1,0:T(8,128)(2,1)}, bf16[1,128,2048]{2,1,0:T(8,128)(2,1)}, bf16[1,128,2048]{2,1,0:T(8,128)(2,1)}) fusion(s32[128]{0:T(128)S(1)} %get-tuple-element.22, s32[128]{0:T(128)S(1)} %get-tuple-element.23), kind=kLoop, calls=%fused_computation.206 | loop fusion | flops 8912896 | bytes 2098176 | tf_op jit(solution)/shard_map/convert.16
  147.3 5.2 %all-to-all-done.1 = bf16[32,2,6144]{2,1,0:T(2,128)(2,1)S(1)} async-done(((bf16[32,2,6144]{2,1,0:T(2,128)(2,1)}), bf16[32,2,6144]{2,1,0:T(2,128)(2,1)S(1)}, u32[]{:S(2)}, u32[]{:S(2)}) %all-to-all-start.1) | async-done | bytes 786464 | tf_op jit(solution)/shard_map/all_to_all | solution.py:69
  152.6 2.7 reshape.1286
  155.2 2.8 bitcast_bitcast_fusion
  158.0 5.3 %copy.27 = bf16[6,1,2,32,32,32]{5,4,3,2,0,1:T(8,128)(2,1)} copy(bf16[6,1,2,32,32,32]{3,5,2,0,1,4:T(8,128)(2,1)S(1)} %bitcast_bitcast_fusion) | data formatting | bytes 1572864 | tf_op jit(solution)/shard_map/reshape | solution.py:70
  163.3 5.0 %reshape.1243 = bf16[6,1,2,32,1024]{4,3,2,0,1:T(8,128)(2,1)S(1)} reshape(bf16[6,1,2,32,32,32]{5,4,3,2,0,1:T(8,128)(2,1)} %copy.27) | data formatting | bytes 1572864 | tf_op jit(solution)/shard_map/reshape | solution.py:70
  168.4 0.4 convolution_bitcast_fusion
  168.8 0.4 convolution_bitcast_fusion.1
  169.2 0.1 copy-done.1
  169.4 0.2 copy-done.2
  169.5 0.4 convolution_bitcast_fusion.2
  170.0 0.4 convolution_bitcast_fusion.3
  170.6 0.4 convolution_bitcast_fusion.4
  171.1 0.2 copy-done.14
  171.2 0.4 convolution_bitcast_fusion.5
  171.6 0.1 copy-done.8
  171.7 0.4 convolution_bitcast_fusion.6
  172.1 0.1 copy-done.16
  172.3 0.8 fusion.15
  173.2 3.3 %collective-permute-start.1 = (f32[2,1,32,2048]{3,2,1,0:T(8,128)S(1)}, f32[2,1,32,2048]{3,2,1,0:T(8,128)S(1)}, u32[]{:S(2)}, u32[]{:S(2)}) collective-permute-start(f32[2,1,32,2048]{3,2,1,0:T(8,128)S(1)} %pad_maximum_fusion.24), channel_id=1, source_target_pairs={{0,1},{1,2},{2,3},{3,4},{4,5},{5,6},{6,7},{7,8},{8,9},{9,10},{10,1... | collective-permute-start | bytes 1572872 | tf_op jit(solution)/shard_map/ppermute | solution.py:21
  176.5 2.2 collective-permute-start
  178.8 2.4 collective-permute-start.3
  181.2 5.0 %collective-permute-start.2 = (f32[2,1,32,2048]{3,2,1,0:T(8,128)S(1)}, f32[2,1,32,2048]{3,2,1,0:T(8,128)S(1)}, u32[]{:S(2)}, u32[]{:S(2)}) collective-permute-start(f32[2,1,32,2048]{3,2,1,0:T(8,128)S(1)} %pad_maximum_fusion.25), channel_id=1, source_target_pairs={{0,1},{1,2},{2,3},{3,4},{4,5},{5,6},{6,7},{7,8},{8,9},{9,10},{10,1... | collective-permute-start | bytes 1572872 | tf_op jit(solution)/shard_map/ppermute | solution.py:21
  186.2 1.3 collective-permute-done.1
  187.5 5.1 %collective-permute-done = f32[2,1,32,2048]{3,2,1,0:T(8,128)S(1)} collective-permute-done((f32[2,1,32,2048]{3,2,1,0:T(8,128)S(1)}, f32[2,1,32,2048]{3,2,1,0:T(8,128)S(1)}, u32[]{:S(2)}, u32[]{:S(2)}) %collective-permute-start) | collective-permute-done | bytes 524320 | tf_op jit(solution)/shard_map/ppermute | solution.py:23
  192.9 11.0 %collective-permute-done.3 = f32[2,1,32,2048]{3,2,1,0:T(8,128)S(1)} collective-permute-done((f32[2,1,32,2048]{3,2,1,0:T(8,128)S(1)}, f32[2,1,32,2048]{3,2,1,0:T(8,128)S(1)}, u32[]{:S(2)}, u32[]{:S(2)}) %collective-permute-start.3) | collective-permute-done | bytes 524320 | tf_op jit(solution)/shard_map/ppermute | solution.py:23
  204.0 0.5 fusion.55
  204.5 0.5 fusion.54
  205.1 0.5 fusion.53
  205.6 0.5 fusion.52
  206.1 0.5 fusion.51
  206.6 0.5 fusion.50
  207.1 0.5 fusion.49
  207.7 0.5 fusion.48
  208.2 1.0 multiply_convert_fusion
  209.2 6.8 %copy.28 = bf16[6,1,2,32,1024]{3,2,1,0,4:T(2,128)(2,1)S(1)} copy(bf16[6,1,2,32,1024]{4,3,0,2,1:T(8,128)(2,1)} %multiply_convert_fusion) | data formatting | bytes 1572864 | tf_op jit(solution)/shard_map/convert_element_type | solution.py:111
  216.0 3.7 %reshape.1287 = bf16[32,2,6144]{2,1,0:T(2,128)(2,1)} reshape(bf16[1024,6,1,2,32]{4,3,2,1,0:T(2,128)(2,1)S(1)} %bitcast.422) | data formatting | bytes 1572864
  219.8 8.9 %all-to-all-start.2 = ((bf16[32,2,6144]{2,1,0:T(2,128)(2,1)}), bf16[32,2,6144]{2,1,0:T(2,128)(2,1)}, u32[]{:S(2)}, u32[]{:S(2)}) async-start(bf16[32,2,6144]{2,1,0:T(2,128)(2,1)} %reshape.1287), calls=%async_computation.2 | async-start | bytes 1572864 | tf_op jit(solution)/shard_map/all_to_all | solution.py:113
  229.3 4.6 %reshape.1253 = f32[4,1,2,1024,32]{3,4,2,0,1:T(8,128)} reshape(f32[4,1,2,32,32,32]{4,3,5,2,0,1:T(8,128)} %get-tuple-element.10) | data formatting | bytes 2097152 | tf_op jit(solution)/shard_map/convert_element_type | solution.py:118
  233.9 39.5 %all-to-all-done.2 = bf16[32,2,6144]{2,1,0:T(2,128)(2,1)} async-done(((bf16[32,2,6144]{2,1,0:T(2,128)(2,1)}), bf16[32,2,6144]{2,1,0:T(2,128)(2,1)}, u32[]{:S(2)}, u32[]{:S(2)}) %all-to-all-start.2) | async-done | bytes 786464 | tf_op jit(solution)/shard_map/all_to_all | solution.py:113
  273.4 7.2 %reshape.1288 = bf16[1024,6,1,2,32]{4,3,2,1,0:T(2,128)(2,1)S(1)} reshape(bf16[32,2,6144]{2,1,0:T(2,128)(2,1)} %all-to-all-done.2) | data formatting | bytes 1572864
  280.6 3.7 %copy.53 = bf16[6,1,2,32,32,32]{3,4,5,2,0,1:T(8,128)(2,1)} copy(bf16[6,1,2,32,32,32]{3,2,0,5,4,1:T(2,128)(2,1)S(1)} %bitcast.420) | data formatting | bytes 1572864 | tf_op jit(solution)/shard_map/all_to_all | solution.py:113
  284.3 5.0 %reshape.1252 = bf16[6,2,1024,32]{2,3,1,0:T(8,128)(2,1)S(1)} reshape(bf16[6,1,2,32,32,32]{4,3,5,2,0,1:T(8,128)(2,1)} %bitcast.421) | data formatting | bytes 1572864 | tf_op jit(solution)/shard_map/reshape.41
  289.3 16.1 %fusion.33 = f32[6,2,32,1024]{3,2,1,0:T(8,128)S(1)} fusion(bf16[6,2,1024,32]{2,3,1,0:T(8,128)(2,1)S(1)} %reshape.1252, s32[1024]{0:T(1024)S(1)} %multiply_add_fusion.1, pred[32,1024]{1,0:T(8,128)(4,1)S(1)} %iota_compare_fusion.1), kind=kOutput, calls=%fused_computation.132 | convolution fusion | flops 821428224 | bytes 2396160 | tf_op jit(solution)/shard_map/crstk,tl->crskl/dot_general | solution.py:115
  305.5 0.8 slice_bitcast_fusion
  306.3 1.1 fusion.82
  (83 shorter events, 4.2 us)
Async XLA Ops:
  13.7 24.6 %copy-start.17 = (s32[1024]{0:T(1024)S(1)}, s32[1024]{0:T(1024)}, u32[]{:S(2)}) copy-start(s32[1024]{0:T(1024)} %param.7) | copy-start | bytes 12292
  13.7 24.8 %copy-start.18 = (bf16[2,1,2,32,1024]{4,3,2,1,0:T(8,128)(2,1)S(1)}, bf16[2,1,2,32,1024]{4,3,2,1,0:T(8,128)(2,1)}, u32[]{:S(2)}) copy-start(bf16[2,1,2,32,1024]{4,3,2,1,0:T(8,128)(2,1)} %param.5) | copy-start | bytes 786436
  21.7 50.0 %all-to-all-start = ((bf16[32,2,4096]{2,1,0:T(2,128)(2,1)}), bf16[32,2,4096]{2,1,0:T(2,128)(2,1)S(1)}, u32[]{:S(2)}, u32[]{:S(2)}) async-start(bf16[32,2,4096]{2,1,0:T(2,128)(2,1)} %reshape.1283), calls=%async_computation | async-start | bytes 1048576 | tf_op jit(solution)/shard_map/all_to_all | solution.py:53
  103.5 49.1 %all-to-all-start.1 = ((bf16[32,2,6144]{2,1,0:T(2,128)(2,1)}), bf16[32,2,6144]{2,1,0:T(2,128)(2,1)S(1)}, u32[]{:S(2)}, u32[]{:S(2)}) async-start(bf16[32,2,6144]{2,1,0:T(2,128)(2,1)} %reshape.1285), calls=%async_computation.1 | async-start | bytes 1572864 | tf_op jit(solution)/shard_map/all_to_all | solution.py:69
  163.3 5.0 %copy-start.3 = (bf16[1,128,2048]{2,1,0:T(8,128)(2,1)S(1)}, bf16[1,128,2048]{2,1,0:T(8,128)(2,1)}, u32[]{:S(2)}) copy-start(bf16[1,128,2048]{2,1,0:T(8,128)(2,1)} %get-tuple-element.38) | copy-start | bytes 1572868
  163.3 5.0 %copy-start.4 = (bf16[1,128,2048]{2,1,0:T(8,128)(2,1)S(1)}, bf16[1,128,2048]{2,1,0:T(8,128)(2,1)}, u32[]{:S(2)}) copy-start(bf16[1,128,2048]{2,1,0:T(8,128)(2,1)} %get-tuple-element.39) | copy-start | bytes 1572868
  163.3 5.5 %copy-start.11 = (bf16[1,128,2048]{2,1,0:T(8,128)(2,1)S(1)}, bf16[1,128,2048]{2,1,0:T(8,128)(2,1)}, u32[]{:S(2)}) copy-start(bf16[1,128,2048]{2,1,0:T(8,128)(2,1)} %get-tuple-element.40) | copy-start | bytes 1572868
  163.3 5.5 %copy-start.12 = (bf16[1,128,2048]{2,1,0:T(8,128)(2,1)S(1)}, bf16[1,128,2048]{2,1,0:T(8,128)(2,1)}, u32[]{:S(2)}) copy-start(bf16[1,128,2048]{2,1,0:T(8,128)(2,1)} %get-tuple-element.41) | copy-start | bytes 1572868
  168.3 1.0 copy-start.1
  168.3 1.2 copy-start.2
  168.8 1.2 copy-start.9
  168.8 1.3 copy-start.10
  169.2 1.3 copy-start.5
  169.2 1.3 copy-start.6
  169.9 1.2 copy-start.13
  169.9 1.3 copy-start.14
  170.4 1.2 copy-start.7
  170.4 1.3 copy-start.8
  170.9 1.2 copy-start.15
  170.9 1.3 copy-start.16
  173.2 14.3 %collective-permute-start.1 = (f32[2,1,32,2048]{3,2,1,0:T(8,128)S(1)}, f32[2,1,32,2048]{3,2,1,0:T(8,128)S(1)}, u32[]{:S(2)}, u32[]{:S(2)}) collective-permute-start(f32[2,1,32,2048]{3,2,1,0:T(8,128)S(1)} %pad_maximum_fusion.24), channel_id=1, source_target_pairs={{0,1},{1,2},{2,3},{3,4},{4,5},{5,6},{6,7},{7,8},{8,9},{9,10},{10,1... | collective-permute-start | bytes 1572872 | tf_op jit(solution)/shard_map/ppermute | solution.py:21
  176.5 16.2 %collective-permute-start = (f32[2,1,32,2048]{3,2,1,0:T(8,128)S(1)}, f32[2,1,32,2048]{3,2,1,0:T(8,128)S(1)}, u32[]{:S(2)}, u32[]{:S(2)}) collective-permute-start(f32[2,1,32,2048]{3,2,1,0:T(8,128)S(1)} %pad_maximum_fusion.24), channel_id=1, source_target_pairs={{1,0},{2,1},{3,2},{4,3},{5,4},{6,5},{7,6},{8,7},{9,8},{10,9},{11,1... | collective-permute-start | bytes 1572872 | tf_op jit(solution)/shard_map/ppermute | solution.py:23
  178.8 25.1 %collective-permute-start.3 = (f32[2,1,32,2048]{3,2,1,0:T(8,128)S(1)}, f32[2,1,32,2048]{3,2,1,0:T(8,128)S(1)}, u32[]{:S(2)}, u32[]{:S(2)}) collective-permute-start(f32[2,1,32,2048]{3,2,1,0:T(8,128)S(1)} %pad_maximum_fusion.25), channel_id=1, source_target_pairs={{1,0},{2,1},{3,2},{4,3},{5,4},{6,5},{7,6},{8,7},{9,8},{10,9},{11,1... | collective-permute-start | bytes 1572872 | tf_op jit(solution)/shard_map/ppermute | solution.py:23
  181.2 22.7 %collective-permute-start.2 = (f32[2,1,32,2048]{3,2,1,0:T(8,128)S(1)}, f32[2,1,32,2048]{3,2,1,0:T(8,128)S(1)}, u32[]{:S(2)}, u32[]{:S(2)}) collective-permute-start(f32[2,1,32,2048]{3,2,1,0:T(8,128)S(1)} %pad_maximum_fusion.25), channel_id=1, source_target_pairs={{0,1},{1,2},{2,3},{3,4},{4,5},{5,6},{6,7},{7,8},{8,9},{9,10},{10,1... | collective-permute-start | bytes 1572872 | tf_op jit(solution)/shard_map/ppermute | solution.py:21
  219.8 53.6 %all-to-all-start.2 = ((bf16[32,2,6144]{2,1,0:T(2,128)(2,1)}), bf16[32,2,6144]{2,1,0:T(2,128)(2,1)}, u32[]{:S(2)}, u32[]{:S(2)}) async-start(bf16[32,2,6144]{2,1,0:T(2,128)(2,1)} %reshape.1287), calls=%async_computation.2 | async-start | bytes 1572864 | tf_op jit(solution)/shard_map/all_to_all | solution.py:113
  289.3 17.0 %copy-start = (f32[4,1,2,1024,32]{3,4,2,0,1:T(8,128)S(1)}, f32[4,1,2,1024,32]{3,4,2,0,1:T(8,128)}, u32[]{:S(2)}) copy-start(f32[4,1,2,1024,32]{3,4,2,0,1:T(8,128)} %reshape.1253) | copy-start | bytes 3145732
